TPU v7x, 32 devices: a whole 2x2x4 slice. The times are simulated.
32 devices in a mesh: groups: 2 (over y), ctx: 16 (over z, x, core).
Axes of the slice: x: 2, y: 2, z: 4, core: 2. Of those that a mesh axis runs over, the one named last changes fastest.
Arguments:
- queries: bfloat16 [4096, 2560], P(('groups', 'ctx')), parts along dimension 0, may hold values from -6 to 6
- key_states: bfloat16 [4096, 2560], P(('groups', 'ctx')), parts along dimension 0, may hold values from -6 to 6
- value_states: bfloat16 [4096, 2560], P(('groups', 'ctx')), parts along dimension 0, may hold values from -6 to 6
- out_grads: bfloat16 [4096, 2560], P(('groups', 'ctx')), parts along dimension 0, may hold values from -6 to 6
- log_norms: bfloat16 [20, 4096], P(None, ('groups', 'ctx')), parts along dimension 1, may hold values from 6.5 to 8.5
- row_deltas: bfloat16 [20, 4096], P(None, ('groups', 'ctx')), parts along dimension 1, may hold values from -24 to 24
- kv_blocks: int32 [16, 7], replicated, may hold values from -1 to 15, as said below
Outputs:
- query_grads: bfloat16 [4096, 2560], P(('groups', 'ctx')), parts along dimension 0
- key_grads: bfloat16 [4096, 2560], P(('groups', 'ctx')), parts along dimension 0
- value_grads: bfloat16 [4096, 2560], P(('groups', 'ctx')), parts along dimension 0
There are 2 independent parts, one for each index of `groups`. A program takes and returns all parts, laid end to end along the dimension named above; an argument that names none is the same for every part. Nothing has to cross between parts.
Inputs may be any that keep to these rules, and one draw needn't show every extreme that they name: `kv_blocks`: row b lists distinct blocks in any order of its slots, the rest -1: the blocks b - 1, b and b + 1 that lie in 0 to 15, and otherwise only blocks whose group index k // 1 differs from b // 1 by + or - 2 ** j with 1 <= j <= 2. For each group of 1 query block and each such other group, at most one entry in all of the group's rows names a block of the other group.
All inputs are finite; a program needn't handle non-finite values.
Results may differ from a plain program's by a relative error of at most 0.0049.
Values may be sent and summed in bfloat16 or wider, within the bound.
A program may use at most 128 MiB of HBM per device.

v0:
```python
import jax
import jax.numpy as jnp
from jax import lax
from jax.sharding import PartitionSpec as P

BLK = 128
LEVELS = 2


def extended(array, sides, width):
    for axis, dim in sides:
        size, length = (lax.axis_size(axis), array.shape[dim])
        up = [(i, (i + 1) % size) for i in range(size - 1)]
        down = [(j, i) for i, j in up]
        last = lax.slice_in_dim(array, length - width, length, axis=dim)
        first = lax.slice_in_dim(array, 0, width, axis=dim)
        before = lax.ppermute(last, axis, up)
        after = lax.ppermute(first, axis, down)
        array = jnp.concatenate([before, array, after], axis=dim)
    return array


def passed_along(block, axis, distance):
    devices = range(lax.axis_size(axis))
    route = [(i - distance, i) for i in devices if i - distance in devices]
    return lax.ppermute(block, axis, route)


def tile_grads(query_tile, grad_tile, norm_tile, delta_tile, key_tile, value_tile, weights):
    head_dim = query_tile.shape[-1]
    factor = head_dim ** (-0.5)
    query_major = query_tile.transpose(1, 0, 2)
    grad_major = grad_tile.transpose(1, 0, 2)
    key_major = key_tile.transpose(1, 0, 2)
    value_major = value_tile.transpose(1, 0, 2)
    scores = (
        jnp.einsum("hqd,hkd->hqk", query_major, key_major, preferred_element_type=jnp.float32)
        * factor
    )
    probs = jnp.exp(scores - norm_tile.astype(jnp.float32)[:, :, None]) * weights[None, None, :]
    probs_low = probs.astype(jnp.bfloat16)
    dprobs = jnp.einsum("hqd,hkd->hqk", grad_major, value_major, preferred_element_type=jnp.float32)
    dscores = (probs * (dprobs - delta_tile.astype(jnp.float32)[:, :, None])).astype(jnp.bfloat16)
    value_part = jnp.einsum(
        "hqk,hqd->khd", probs_low, grad_major, preferred_element_type=jnp.float32
    )
    key_part = (
        jnp.einsum("hqk,hqd->khd", dscores, query_major, preferred_element_type=jnp.float32)
        * factor
    )
    query_part = (
        jnp.einsum("hqk,hkd->qhd", dscores, key_major, preferred_element_type=jnp.float32) * factor
    )
    return (query_part, key_part, value_part)


def per_device(queries, key_states, value_states, out_grads, log_norms, row_deltas, kv_blocks):
    tok_rows, width = queries.shape
    heads = log_norms.shape[0]
    head_dim = width // heads
    blocks_dev = tok_rows // BLK
    devices = lax.axis_size("ctx")
    here = lax.axis_index("ctx")
    all_blocks = blocks_dev * devices
    query_blk = queries.reshape(blocks_dev, BLK, heads, head_dim)
    grad_blk = out_grads.reshape(blocks_dev, BLK, heads, head_dim)
    norm_blk = log_norms.reshape(heads, blocks_dev, BLK).transpose(1, 0, 2)
    delta_blk = row_deltas.reshape(heads, blocks_dev, BLK).transpose(1, 0, 2)
    stacked = jnp.stack([key_states, value_states])
    widened = extended(stacked, (("ctx", 1),), BLK)
    ext_keys = widened[0].reshape(blocks_dev + 2, BLK, heads, head_dim)
    ext_values = widened[1].reshape(blocks_dev + 2, BLK, heads, head_dim)
    band_keys = jnp.concatenate(
        [ext_keys[shift_idx : shift_idx + blocks_dev] for shift_idx in range(3)], axis=1
    )
    band_values = jnp.concatenate(
        [ext_values[shift_idx : shift_idx + blocks_dev] for shift_idx in range(3)], axis=1
    )
    block_ids = (
        here * blocks_dev
        + jnp.arange(blocks_dev, dtype=jnp.int32)[:, None]
        + jnp.arange(3, dtype=jnp.int32)[None, :]
        - 1
    )
    inside = ((block_ids >= 0) & (block_ids < all_blocks)).astype(jnp.float32)
    band_weights = jnp.repeat(inside, BLK, axis=1)
    band_query, band_key, band_value = jax.vmap(tile_grads)(
        query_blk, grad_blk, norm_blk, delta_blk, band_keys, band_values, band_weights
    )
    ext_dk = jnp.zeros((blocks_dev + 2, BLK, heads, head_dim), jnp.float32)
    ext_dv = jnp.zeros((blocks_dev + 2, BLK, heads, head_dim), jnp.float32)
    for shift_idx in range(3):
        ext_dk = ext_dk.at[shift_idx : shift_idx + blocks_dev].add(
            band_key[:, shift_idx * BLK : (shift_idx + 1) * BLK]
        )
        ext_dv = ext_dv.at[shift_idx : shift_idx + blocks_dev].add(
            band_value[:, shift_idx * BLK : (shift_idx + 1) * BLK]
        )
    kv_acc = jnp.stack(
        [ext_dk[1:-1].reshape(tok_rows, width), ext_dv[1:-1].reshape(tok_rows, width)]
    )
    rims = jnp.stack(
        [jnp.concatenate([ext_dk[0], ext_dk[-1]]), jnp.concatenate([ext_dv[0], ext_dv[-1]])]
    ).reshape(2, 2 * BLK, width)
    returned = extended(rims, (("ctx", 1),), BLK)
    kv_acc = kv_acc.at[:, :BLK].add(returned[:, :BLK])
    kv_acc = kv_acc.at[:, tok_rows - BLK :].add(returned[:, 3 * BLK :])
    query_acc = band_query.reshape(tok_rows, width)

    def pick(query_dev, key_dev):
        start = jnp.clip(query_dev, 0, devices - 1) * blocks_dev
        listed = lax.dynamic_slice_in_dim(kv_blocks, start, blocks_dev, 0)
        matches = ((listed >= 0) & (listed // blocks_dev == key_dev)).astype(jnp.int32)
        usable = (
            (query_dev >= 0) & (query_dev < devices) & (key_dev >= 0) & (key_dev < devices)
        ).astype(jnp.int32)
        present = jnp.max(matches) * usable
        query_pos = jnp.sum(matches * jnp.arange(blocks_dev, dtype=jnp.int32)[:, None])
        key_pos = jnp.sum(matches * (listed % blocks_dev))
        return (present, query_pos, key_pos)

    def kv_piece(position):
        return lax.dynamic_index_in_dim(
            stacked.reshape(2, blocks_dev, BLK, width), position, 1, False
        )

    def send(offset):
        present, query_pos, key_pos = pick(here - offset, here)
        return passed_along(kv_piece(key_pos), "ctx", -offset)

    offsets = [
        direction * 2**rung_idx for rung_idx in range(1, LEVELS + 1) for direction in (1, -1)
    ]
    arrivals = [send(offset) for offset in offsets]
    leaving = []
    for offset, received in zip(offsets, arrivals):
        work_query_total = query_acc
        work_present, work_query_pos, work_key_pos = pick(here, here + offset)
        query_pair = jnp.stack(
            [
                lax.dynamic_index_in_dim(
                    queries.reshape(blocks_dev, BLK, width), work_query_pos, 0, False
                ),
                lax.dynamic_index_in_dim(
                    out_grads.reshape(blocks_dev, BLK, width), work_query_pos, 0, False
                ),
            ]
        )
        query_stats = jnp.stack(
            [
                lax.dynamic_index_in_dim(norm_blk, work_query_pos, 0, False),
                lax.dynamic_index_in_dim(delta_blk, work_query_pos, 0, False),
            ]
        )
        weights = jnp.ones((BLK,), jnp.float32) * work_present.astype(jnp.float32)
        part_q, part_k, part_v = tile_grads(
            query_pair[0].reshape(BLK, heads, head_dim),
            query_pair[1].reshape(BLK, heads, head_dim),
            query_stats[0],
            query_stats[1],
            received[0].reshape(BLK, heads, head_dim),
            received[1].reshape(BLK, heads, head_dim),
            weights,
        )
        add_current = work_query_total
        work_query_total = add_current + part_q.reshape(BLK, width)
        work_outgoing = jnp.stack([part_k.reshape(BLK, width), part_v.reshape(BLK, width)])
        query_acc, kv_acc, outgoing = (work_query_total, kv_acc, work_outgoing)
        leaving.append(outgoing)
    for offset, outgoing in zip(offsets, leaving):
        kv_total = kv_acc
        arrived = passed_along(outgoing, "ctx", offset)
        current = kv_total
        kv_total = current + arrived
        query_acc, kv_acc = (query_acc, kv_total)
    return (
        query_acc.astype(jnp.bfloat16),
        kv_acc[0].astype(jnp.bfloat16),
        kv_acc[1].astype(jnp.bfloat16),
    )


def solution(mesh):
    return jax.shard_map(
        per_device,
        mesh=mesh,
        in_specs=(
            P(("groups", "ctx"), None),
            P(("groups", "ctx"), None),
            P(("groups", "ctx"), None),
            P(("groups", "ctx"), None),
            P(None, ("groups", "ctx")),
            P(None, ("groups", "ctx")),
            P(),
        ),
        out_specs=(
            P(("groups", "ctx"), None),
            P(("groups", "ctx"), None),
            P(("groups", "ctx"), None),
        ),
        check_vma=False,
    )
```

profile of v0, /device:TPU:1, one launch (start us, length us, event | category | flops | bytes accessed | tf_op | source)
XLA Modules:
  0.0 357.0 jit_solution(15789150595436192082)
XLA Ops:
  0.6 1.5 copy.47
  3.7 5.2 %collective-permute-start.5 = (bf16[2,128,2560]{1,2,0:T(8,128)(2,1)}, bf16[2,128,2560]{1,2,0:T(8,128)(2,1)}, u32[]{:S(2)}, u32[]{:S(2)}) collective-permute-start(bf16[2,128,2560]{1,2,0:T(8,128)(2,1)} %pad_maximum_fusion.4), channel_id=1, source_target_pairs={{0,4},{1,5},{2,6},{3,7},{4,8},{5,9},{6,10},{7,11},{8,12},{9,13},{1... | collective-permute-start | bytes 3932168 | tf_op jit(solution)/shard_map/ppermute | solution.py:26
  10.2 4.3 %collective-permute-start.3 = (bf16[2,128,2560]{1,2,0:T(8,128)(2,1)}, bf16[2,128,2560]{1,2,0:T(8,128)(2,1)}, u32[]{:S(2)}, u32[]{:S(2)}) collective-permute-start(bf16[2,128,2560]{1,2,0:T(8,128)(2,1)} %pad_maximum_fusion.4), channel_id=1, source_target_pairs={{0,2},{1,3},{2,4},{3,5},{4,6},{5,7},{6,8},{7,9},{8,10},{9,11},{10,... | collective-permute-start | bytes 3932168 | tf_op jit(solution)/shard_map/ppermute | solution.py:26
  14.4 3.1 collective-permute-start.1
  17.6 3.0 collective-permute-start
  26.9 8.7 %collective-permute-done.5 = bf16[2,128,2560]{1,2,0:T(8,128)(2,1)} collective-permute-done((bf16[2,128,2560]{1,2,0:T(8,128)(2,1)}, bf16[2,128,2560]{1,2,0:T(8,128)(2,1)}, u32[]{:S(2)}, u32[]{:S(2)}) %collective-permute-start.5) | collective-permute-done | bytes 1310752 | tf_op jit(solution)/shard_map/ppermute | solution.py:26
  36.9 2.2 fusion.68
  40.4 2.2 fusion.67
  42.6 2.4 fusion.66
  48.4 1.5 fusion.22
  49.9 1.6 fusion.48
  51.9 1.6 fusion.50
  53.6 2.4 fusion.65
  56.0 42.4 %collective-permute-done = bf16[2,128,2560]{1,2,0:T(8,128)(2,1)} collective-permute-done((bf16[2,128,2560]{1,2,0:T(8,128)(2,1)}, bf16[2,128,2560]{1,2,0:T(8,128)(2,1)}, u32[]{:S(2)}, u32[]{:S(2)}) %collective-permute-start) | collective-permute-done | bytes 1310752 | tf_op jit(solution)/shard_map/ppermute | solution.py:17
  98.4 2.4 fusion.64
  100.8 1.5 fusion.30
  102.4 2.2 copy.84
  104.5 2.2 copy.78
  106.7 2.2 copy.72
  108.8 2.2 copy.51
  111.0 2.2 copy.49
  113.2 2.2 copy.57
  115.5 2.2 copy.55
  117.6 3.1 fusion.52
  124.5 2.2 fusion.63
  127.8 2.2 copy.64
  130.0 1.5 fusion.34
  131.5 1.7 fusion.54
  134.3 1.7 fusion.15
  136.0 2.8 copy.99
  138.8 3.5 pad_maximum_fusion.3
  142.3 1.5 collective-permute-start.11
  143.8 1.7 fusion.16
  145.5 2.8 copy.97
  148.3 3.3 pad_maximum_fusion.2
  151.6 6.2 %collective-permute-start.10 = (f32[2,128,2560]{1,2,0:T(8,128)}, f32[2,128,2560]{1,2,0:T(8,128)}, u32[]{:S(2)}, u32[]{:S(2)}) collective-permute-start(f32[2,128,2560]{1,2,0:T(8,128)} %pad_maximum_fusion.2), channel_id=1, source_target_pairs={{0,4},{1,5},{2,6},{3,7},{4,8},{5,9},{6,10},{7,11},{8,12},{9,13},{1... | collective-permute-start | bytes 7864328 | tf_op jit(solution)/shard_map/ppermute | solution.py:26
  157.8 1.6 fusion.17
  159.5 2.8 copy.95
  162.3 3.4 pad_maximum_fusion.1
  167.0 1.7 fusion.18
  168.6 2.8 copy.93
  171.4 3.5 pad_maximum_fusion
  174.9 5.6 %collective-permute-start.8 = (f32[2,128,2560]{1,2,0:T(8,128)}, f32[2,128,2560]{1,2,0:T(8,128)}, u32[]{:S(2)}, u32[]{:S(2)}) collective-permute-start(f32[2,128,2560]{1,2,0:T(8,128)} %pad_maximum_fusion), channel_id=1, source_target_pairs={{0,2},{1,3},{2,4},{3,5},{4,6},{5,7},{6,8},{7,9},{8,10},{9,11},{10,... | collective-permute-start | bytes 7864328 | tf_op jit(solution)/shard_map/ppermute | solution.py:26
  181.2 2.8 multiply_convert_fusion
  185.4 2.1 fusion.61
  187.5 2.8 copy.91
  190.3 2.8 copy.90
  193.1 3.1 convolution_bitcast_fusion
  196.3 1.4 fusion.62
  198.9 2.7 fusion.60
  201.6 4.5 %collective-permute-start.7 = (f32[2,128,2560]{1,2,0:T(8,128)}, f32[2,128,2560]{1,2,0:T(8,128)}, u32[]{:S(2)}, u32[]{:S(2)}) collective-permute-start(f32[2,128,2560]{1,2,0:T(8,128)} %get-tuple-element.123), channel_id=1, source_target_pairs={{1,0},{2,1},{3,2},{4,3},{5,4},{6,5},{7,6},{8,7},{9,8},{10,9},{11,1... | collective-permute-start | bytes 7864328 | tf_op jit(solution)/shard_map/ppermute | solution.py:18
  206.1 3.2 collective-permute-start.6
  210.8 2.9 copy.87
  213.7 1.5 convolution_multiply_fusion.7
  215.1 2.8 copy.81
  218.3 1.5 copy.75
  219.9 2.5 convolution_multiply_fusion
  222.4 1.5 copy.68
  224.2 1.5 copy.69
  225.7 1.8 copy.89
  227.5 3.9 %add_convert_fusion = bf16[128,2560]{1,0:T(8,128)(2,1)} fusion(f32[128,2560]{1,0:T(8,128)S(1)} %copy-done.15, f32[128,2560]{1,0:T(8,128)} %copy.81, f32[128,2560]{1,0:T(8,128)} %copy.75, f32[128,2560]{1,0:T(8,128)} %copy.68, f32[128,2560]{1,0:T(8,128)} %copy.69), kind=kLoop, calls=%fused_computation.68 | loop fusion | flops 1638400 | bytes 7208960 | tf_op jit(solution)/shard_map/convert_element_type | solution.py:177
  231.4 86.0 %collective-permute-done.8 = f32[2,128,2560]{1,2,0:T(8,128)} collective-permute-done((f32[2,128,2560]{1,2,0:T(8,128)}, f32[2,128,2560]{1,2,0:T(8,128)}, u32[]{:S(2)}, u32[]{:S(2)}) %collective-permute-start.8) | collective-permute-done | bytes 2621472 | tf_op jit(solution)/shard_map/ppermute | solution.py:26
  317.4 31.0 %collective-permute-done.6 = f32[2,128,2560]{1,2,0:T(8,128)} collective-permute-done((f32[2,128,2560]{1,2,0:T(8,128)}, f32[2,128,2560]{1,2,0:T(8,128)}, u32[]{:S(2)}, u32[]{:S(2)}) %collective-permute-start.6) | collective-permute-done | bytes 2621472 | tf_op jit(solution)/shard_map/ppermute | solution.py:17
  348.4 6.3 %fusion.6 = bf16[2,128,2560]{1,2,0:T(8,128)(2,1)S(1)} fusion(f32[2,128,2560]{1,2,0:T(8,128)} %collective-permute-done.11, f32[2,128,2560]{1,2,0:T(8,128)} %collective-permute-done.10, f32[2,128,2560]{1,2,0:T(8,128)} %collective-permute-done.9, f32[2,128,2560]{1,2,0:T(8,128)} %collective-permute-done.8, f32[2,128,2560]{1,2,0:T(8,128)} %collective-permute-done.7, ...), kind=kLoop, calls=%fused_computation.11 | loop fusion | flops 5242880 | bytes 19660800 | tf_op jit(solution)/shard_map/convert.1
  (118 shorter events, 27.7 us)
Async XLA Ops:
  0.6 1.5 copy-start.30
  2.5 18.2 %copy-start.31 = (bf16[128,2560]{1,0:T(8,128)(2,1)S(1)}, bf16[128,2560]{1,0:T(8,128)(2,1)}, u32[]{:S(2)}) copy-start(bf16[128,2560]{1,0:T(8,128)(2,1)} %param.27) | copy-start | bytes 1966084
  3.7 17.3 %copy-start.38 = (s32[16,7]{0,1:T(8,128)S(1)}, s32[16,7]{0,1:T(8,128)}, u32[]{:S(2)}) copy-start(s32[16,7]{0,1:T(8,128)} %param.33) | copy-start | bytes 1348
  3.7 18.7 %copy-start.36 = (bf16[20,128]{1,0:T(8,128)(2,1)S(1)}, bf16[20,128]{1,0:T(8,128)(2,1)}, u32[]{:S(2)}) copy-start(bf16[20,128]{1,0:T(8,128)(2,1)} %param.31) | copy-start | bytes 15364
  3.7 18.7 %copy-start.32 = (bf16[128,2560]{1,0:T(8,128)(2,1)S(1)}, bf16[128,2560]{1,0:T(8,128)(2,1)}, u32[]{:S(2)}) copy-start(bf16[128,2560]{1,0:T(8,128)(2,1)} %param.30) | copy-start | bytes 1966084
  3.7 31.9 %collective-permute-start.5 = (bf16[2,128,2560]{1,2,0:T(8,128)(2,1)}, bf16[2,128,2560]{1,2,0:T(8,128)(2,1)}, u32[]{:S(2)}, u32[]{:S(2)}) collective-permute-start(bf16[2,128,2560]{1,2,0:T(8,128)(2,1)} %pad_maximum_fusion.4), channel_id=1, source_target_pairs={{0,4},{1,5},{2,6},{3,7},{4,8},{5,9},{6,10},{7,11},{8,12},{9,13},{1... | collective-permute-start | bytes 3932168 | tf_op jit(solution)/shard_map/ppermute | solution.py:26
  8.9 31.5 %collective-permute-start.4 = (bf16[2,128,2560]{1,2,0:T(8,128)(2,1)}, bf16[2,128,2560]{1,2,0:T(8,128)(2,1)}, u32[]{:S(2)}, u32[]{:S(2)}) collective-permute-start(bf16[2,128,2560]{1,2,0:T(8,128)(2,1)} %pad_maximum_fusion.4), channel_id=1, source_target_pairs={{4,0},{5,1},{6,2},{7,3},{8,4},{9,5},{10,6},{11,7},{12,8},{13,9},{1... | collective-permute-start | bytes 3932168 | tf_op jit(solution)/shard_map/ppermute | solution.py:26
  10.2 32.4 %collective-permute-start.3 = (bf16[2,128,2560]{1,2,0:T(8,128)(2,1)}, bf16[2,128,2560]{1,2,0:T(8,128)(2,1)}, u32[]{:S(2)}, u32[]{:S(2)}) collective-permute-start(bf16[2,128,2560]{1,2,0:T(8,128)(2,1)} %pad_maximum_fusion.4), channel_id=1, source_target_pairs={{0,2},{1,3},{2,4},{3,5},{4,6},{5,7},{6,8},{7,9},{8,10},{9,11},{10,... | collective-permute-start | bytes 3932168 | tf_op jit(solution)/shard_map/ppermute | solution.py:26
  14.4 39.1 %collective-permute-start.1 = (bf16[2,128,2560]{1,2,0:T(8,128)(2,1)}, bf16[2,128,2560]{1,2,0:T(8,128)(2,1)}, u32[]{:S(2)}, u32[]{:S(2)}) collective-permute-start(bf16[2,128,2560]{1,2,0:T(8,128)(2,1)} %pad_maximum_fusion.4), channel_id=1, source_target_pairs={{1,0},{2,1},{3,2},{4,3},{5,4},{6,5},{7,6},{8,7},{9,8},{10,9},{11,1... | collective-permute-start | bytes 3932168 | tf_op jit(solution)/shard_map/ppermute | solution.py:18
  17.6 80.8 %collective-permute-start = (bf16[2,128,2560]{1,2,0:T(8,128)(2,1)}, bf16[2,128,2560]{1,2,0:T(8,128)(2,1)}, u32[]{:S(2)}, u32[]{:S(2)}) collective-permute-start(bf16[2,128,2560]{1,2,0:T(8,128)(2,1)} %pad_maximum_fusion.4), channel_id=1, source_target_pairs={{0,1},{1,2},{2,3},{3,4},{4,5},{5,6},{6,7},{7,8},{8,9},{9,10},{10,1... | collective-permute-start | bytes 3932168 | tf_op jit(solution)/shard_map/ppermute | solution.py:17
  20.7 2.1 copy-start.37
  35.6 88.9 %collective-permute-start.2 = (bf16[2,128,2560]{1,2,0:T(8,128)(2,1)}, bf16[2,128,2560]{1,2,0:T(8,128)(2,1)}, u32[]{:S(2)}, u32[]{:S(2)}) collective-permute-start(bf16[2,128,2560]{1,2,0:T(8,128)(2,1)} %pad_maximum_fusion.4), channel_id=1, source_target_pairs={{2,0},{3,1},{4,2},{5,3},{6,4},{7,5},{8,6},{9,7},{10,8},{11,9},{12,... | collective-permute-start | bytes 3932168 | tf_op jit(solution)/shard_map/ppermute | solution.py:26
  42.6 3.6 copy-start.4
  45.1 2.2 copy-start.6
  49.9 1.6 copy-start.27
  51.9 1.6 copy-start.1
  56.0 44.8 %copy-start.23 = (bf16[128,20,128]{2,0,1:T(8,128)(2,1)S(1)}, bf16[128,20,128]{2,0,1:T(8,128)(2,1)}, u32[]{:S(2)}) copy-start(bf16[128,20,128]{2,0,1:T(8,128)(2,1)} %copy.70) | copy-start | bytes 1966084
  117.6 3.1 copy-start.24
  120.7 1.4 copy-start.2
  120.7 1.7 copy-start.25
  122.4 1.4 copy-start.3
  122.4 1.7 copy-start.26
  131.5 1.7 copy-start.28
  133.2 1.2 copy-start.10
  138.8 5.0 %copy-start.8 = (bf16[20,128,128]{2,1,0:T(8,128)(2,1)S(1)}, bf16[20,128,128]{2,1,0:T(8,128)(2,1)}, u32[]{:S(2)}) copy-start(bf16[20,128,128]{2,1,0:T(8,128)(2,1)} %fusion.37) | copy-start | bytes 1966084
  142.3 63.8 %collective-permute-start.11 = (f32[2,128,2560]{1,2,0:T(8,128)}, f32[2,128,2560]{1,2,0:T(8,128)}, u32[]{:S(2)}, u32[]{:S(2)}) collective-permute-start(f32[2,128,2560]{1,2,0:T(8,128)} %pad_maximum_fusion.3), channel_id=1, source_target_pairs={{4,0},{5,1},{6,2},{7,3},{8,4},{9,5},{10,6},{11,7},{12,8},{13,9},{1... | collective-permute-start | bytes 7864328 | tf_op jit(solution)/shard_map/ppermute | solution.py:26
  151.6 79.7 %collective-permute-start.10 = (f32[2,128,2560]{1,2,0:T(8,128)}, f32[2,128,2560]{1,2,0:T(8,128)}, u32[]{:S(2)}, u32[]{:S(2)}) collective-permute-start(f32[2,128,2560]{1,2,0:T(8,128)} %pad_maximum_fusion.2), channel_id=1, source_target_pairs={{0,4},{1,5},{2,6},{3,7},{4,8},{5,9},{6,10},{7,11},{8,12},{9,13},{1... | collective-permute-start | bytes 7864328 | tf_op jit(solution)/shard_map/ppermute | solution.py:26
  162.3 4.7 %copy-start.12 = (bf16[20,128,128]{2,1,0:T(8,128)(2,1)S(1)}, bf16[20,128,128]{2,1,0:T(8,128)(2,1)}, u32[]{:S(2)}) copy-start(bf16[20,128,128]{2,1,0:T(8,128)(2,1)} %fusion.35) | copy-start | bytes 1966084
  165.7 65.7 %collective-permute-start.9 = (f32[2,128,2560]{1,2,0:T(8,128)}, f32[2,128,2560]{1,2,0:T(8,128)}, u32[]{:S(2)}, u32[]{:S(2)}) collective-permute-start(f32[2,128,2560]{1,2,0:T(8,128)} %pad_maximum_fusion.1), channel_id=1, source_target_pairs={{2,0},{3,1},{4,2},{5,3},{6,4},{7,5},{8,6},{9,7},{10,8},{11,9},{12,... | collective-permute-start | bytes 7864328 | tf_op jit(solution)/shard_map/ppermute | solution.py:26
  171.4 9.1 %copy-start.18 = (bf16[1,128,20,128]{3,1,2,0:T(8,128)(2,1)S(1)}, bf16[1,128,20,128]{3,1,2,0:T(8,128)(2,1)}, u32[]{:S(2)}) copy-start(bf16[1,128,20,128]{3,1,2,0:T(8,128)(2,1)} %copy.50) | copy-start | bytes 1966084
  171.4 9.1 %copy-start.20 = (bf16[1,128,20,128]{3,1,2,0:T(8,128)(2,1)S(1)}, bf16[1,128,20,128]{3,1,2,0:T(8,128)(2,1)}, u32[]{:S(2)}) copy-start(bf16[1,128,20,128]{3,1,2,0:T(8,128)(2,1)} %copy.51) | copy-start | bytes 1966084
  171.4 9.1 %copy-start.22 = (bf16[1,128,20,128]{3,1,2,0:T(8,128)(2,1)S(1)}, bf16[1,128,20,128]{3,1,2,0:T(8,128)(2,1)}, u32[]{:S(2)}) copy-start(bf16[1,128,20,128]{3,1,2,0:T(8,128)(2,1)} %copy.49) | copy-start | bytes 1966084
  174.9 6.3 %copy-start.33 = (bf16[1,128,20,128]{3,1,2,0:T(8,128)(2,1)S(1)}, bf16[1,128,20,128]{3,1,2,0:T(8,128)(2,1)}, u32[]{:S(2)}) copy-start(bf16[1,128,20,128]{3,1,2,0:T(8,128)(2,1)} %copy.56) | copy-start | bytes 1966084
  174.9 6.3 %copy-start.34 = (bf16[1,128,20,128]{3,1,2,0:T(8,128)(2,1)S(1)}, bf16[1,128,20,128]{3,1,2,0:T(8,128)(2,1)}, u32[]{:S(2)}) copy-start(bf16[1,128,20,128]{3,1,2,0:T(8,128)(2,1)} %copy.57) | copy-start | bytes 1966084
  174.9 6.3 %copy-start.35 = (bf16[1,128,20,128]{3,1,2,0:T(8,128)(2,1)S(1)}, bf16[1,128,20,128]{3,1,2,0:T(8,128)(2,1)}, u32[]{:S(2)}) copy-start(bf16[1,128,20,128]{3,1,2,0:T(8,128)(2,1)} %copy.55) | copy-start | bytes 1966084
  174.9 142.5 %collective-permute-start.8 = (f32[2,128,2560]{1,2,0:T(8,128)}, f32[2,128,2560]{1,2,0:T(8,128)}, u32[]{:S(2)}, u32[]{:S(2)}) collective-permute-start(f32[2,128,2560]{1,2,0:T(8,128)} %pad_maximum_fusion), channel_id=1, source_target_pairs={{0,2},{1,3},{2,4},{3,5},{4,6},{5,7},{6,8},{7,9},{8,10},{9,11},{10,... | collective-permute-start | bytes 7864328 | tf_op jit(solution)/shard_map/ppermute | solution.py:26
  181.2 2.8 copy-start
  184.1 1.3 copy-start.29
  196.2 1.5 copy-start.16
  196.2 2.2 copy-start.17
  198.8 10.5 %copy-start.11 = (bf16[20,128,128]{2,1,0:T(8,128)(2,1)S(1)}, bf16[20,128,128]{2,1,0:T(8,128)(2,1)}, u32[]{:S(2)}) copy-start(bf16[20,128,128]{2,1,0:T(8,128)(2,1)} %fusion.38) | copy-start | bytes 1966084
  201.6 115.8 %collective-permute-start.7 = (f32[2,128,2560]{1,2,0:T(8,128)}, f32[2,128,2560]{1,2,0:T(8,128)}, u32[]{:S(2)}, u32[]{:S(2)}) collective-permute-start(f32[2,128,2560]{1,2,0:T(8,128)} %get-tuple-element.123), channel_id=1, source_target_pairs={{1,0},{2,1},{3,2},{4,3},{5,4},{6,5},{7,6},{8,7},{9,8},{10,9},{11,1... | collective-permute-start | bytes 7864328 | tf_op jit(solution)/shard_map/ppermute | solution.py:18
  206.1 142.2 %collective-permute-start.6 = (f32[2,128,2560]{1,2,0:T(8,128)}, f32[2,128,2560]{1,2,0:T(8,128)}, u32[]{:S(2)}, u32[]{:S(2)}) collective-permute-start(f32[2,128,2560]{1,2,0:T(8,128)} %get-tuple-element.122), channel_id=1, source_target_pairs={{0,1},{1,2},{2,3},{3,4},{4,5},{5,6},{6,7},{7,8},{8,9},{9,10},{10,1... | collective-permute-start | bytes 7864328 | tf_op jit(solution)/shard_map/ppermute | solution.py:17
  210.8 2.9 copy-start.5
  210.8 2.9 copy-start.9
  215.1 2.8 copy-start.7
  218.3 1.6 copy-start.19
  218.3 1.6 copy-start.21
  222.4 1.5 copy-start.13
  225.7 1.8 copy-start.15
  227.5 120.9 %copy-start.14 = (f32[1,128,20,128]{1,3,2,0:T(8,128)S(1)}, f32[1,128,20,128]{1,3,2,0:T(8,128)}, u32[]{:S(2)}) copy-start(f32[1,128,20,128]{1,3,2,0:T(8,128)} %get-tuple-element.127) | copy-start | bytes 3932164
where the time goes:
time: 359 us; the launch traced here: 357 us
  waiting for transfers between devices  169 us (47%)
  local copies, waits for them, and re-layouts  80.4 us (22%)
  starting transfers between devices  40.5 us (11%)
  matrix products  36.7 us (10%)
  other arithmetic  26.3 us (7%)
  between operations  3.69 us (1%)
    ppermute x8, waiting for transfers between devices, passed_along(): return lax.ppermute(block, axis, route)  96 us
    ppermute x2, waiting for transfers between devices, extended(): before = lax.ppermute(last, axis, up)  73.3 us
    ppermute x8, starting transfers between devices, passed_along(): return lax.ppermute(block, axis, route)  26.6 us
    another operation x4, other arithmetic, per_device(): jnp.stack([part_k.reshape(BLK, width), part_v.reshape(BLK, width)])  13.7 us
    mul x4, local copies, waits for them, and re-layouts, tile_grads(): jnp.einsum('hqk,hqd->khd', dscores, query_major, preferred_element_type=j...  11.2 us
    dot_general x5, matrix products, tile_grads(): jnp.einsum('hqk,hqd->khd', probs_low, grad_major, preferred_element_type=...  11.2 us
    slice x5, local copies, waits for them, and re-layouts, per_device(): ext_values[shift_idx:shift_idx + blocks_dev]  10.4 us
    slice x4, local copies, waits for them, and re-layouts, per_device(): band_key[:, shift_idx * BLK:(shift_idx + 1) * BLK]  9.53 us
  transfers between devices with their start and end apart: 12, of which 5 were waited for; matrix products, arithmetic and copies ran while one was open for 31% of the time, Pallas kernels for 0%

commit v1 on v0

v1 whole, which is shorter than its diff:
```python
import functools

import jax
import jax.numpy as jnp
from jax import lax
from jax.experimental import pallas as pl
from jax.experimental.pallas import tpu as pltpu
from jax.sharding import PartitionSpec as P

BLK = 128
PACK = 2
FAR = 1.0e30

OWN, SIB, CROSS, RELAY, EDGE, TO, FROM = range(7)
SLOTS = 7
(G_SIB, G_CROSS, G_TO, G_FROM, G_RELAY1, G_RELAY2, G_EDGE,
 R_SIB, R_EDGE, R_FROM, R_RELAY1, R_RELAY2, R_CROSS, R_TO) = range(14)
KINDS = 14
NN = (((1,), (0,)), ((), ()))
NT = (((1,), (1,)), ((), ()))
TN = (((0,), (0,)), ((), ()))
MESH = pl.DeviceIdType.MESH


def kernel(devices, heads, q_hbm, k_hbm, v_hbm, g_hbm, stats_in, bias_ref, dq_hbm, dk_hbm, dv_hbm,
           buf, kv, stats, own_acc, cross_acc, relay_acc, to_acc, outgoing, returned, results,
           send_sem, recv_sem, stat_send, stat_recv, local_sem):
    group = lax.axis_index("groups")
    me = lax.axis_index("ctx")
    chunks = heads // PACK
    wide = PACK * 128
    core = me % 2
    chip_odd = (me // 2) % 2
    sign = 1 - 2 * chip_odd
    sib = me + 1 - 2 * core
    cross = me + 2 * sign
    relay = me - 2 * sign
    edge = me + 2 * core - 1
    to = me + 4 * sign
    frm = me - 4 * sign
    has_to = (to >= 0) & (to < devices)
    has_from = (frm >= 0) & (frm < devices)
    has_edge = (edge >= 0) & (edge < devices)
    sib_edge = sib - 2 * core + 1
    has_sib_edge = (sib_edge >= 0) & (sib_edge < devices)
    gives_cross = chip_odd == core
    factor = 128 ** (-0.5)

    def there(device):
        return (group, device)

    places = ((SIB, sib, None), (CROSS, cross, None), (RELAY, relay, has_from),
              (EDGE, edge, has_edge), (TO, to, has_to), (FROM, frm, has_from))
    mirror = {SIB: SIB, CROSS: CROSS, RELAY: RELAY, EDGE: EDGE, TO: FROM, FROM: TO}

    def guarded(condition, action):
        if condition is None:
            action()
        else:
            pl.when(condition)(action)

    loads = [pltpu.make_async_copy(source, target, local_sem.at[n]) for n, (source, target) in enumerate((
        (q_hbm, buf.at[0, pl.ds(0, BLK), :]), (g_hbm, buf.at[1, pl.ds(0, BLK), :]),
        (k_hbm, kv.at[0]), (v_hbm, kv.at[1])))]
    for load in loads:
        load.start()

    barrier = pltpu.get_barrier_semaphore()
    for _, device, present in places:
        guarded(present, lambda device=device: pl.semaphore_signal(
            barrier, inc=1, device_id=there(device), device_id_type=MESH))

    def blank(slot):
        buf[:, pl.ds(slot * BLK, BLK), :] = jnp.zeros((2, BLK, buf.shape[2]), buf.dtype)
        stats[slot] = jnp.zeros(stats.shape[1:], stats.dtype)

    for slot, _, present in places:
        if present is not None:
            pl.when(jnp.logical_not(present))(functools.partial(blank, slot))

    peers = 2 + sum(present.astype(jnp.int32) for _, _, present in places if present is not None)
    pl.semaphore_wait(barrier, peers)

    def stat_copy(slot, device):
        return pltpu.make_async_remote_copy(
            src_ref=stats_in, dst_ref=stats.at[mirror[slot]], send_sem=stat_send.at[slot],
            recv_sem=stat_recv.at[mirror[slot]], device_id=there(device), device_id_type=MESH)

    for slot, device, present in places:
        guarded(present, lambda slot=slot, device=device: stat_copy(slot, device).start())

    def columns(start, size):
        return pl.ds(pl.multiple_of(start, 128), size)

    def moved(kind, from_slot, to_slot, device, j, start, size):
        where = columns(start, size)
        return pltpu.make_async_remote_copy(
            src_ref=buf.at[:, pl.ds(from_slot * BLK, BLK), where],
            dst_ref=buf.at[:, pl.ds(to_slot * BLK, BLK), where],
            send_sem=send_sem.at[kind], recv_sem=recv_sem.at[kind, j],
            device_id=there(device), device_id_type=MESH)

    def handed(kind, slot, to_slot, device, j, start, size):
        where = columns(start, size)
        return pltpu.make_async_remote_copy(
            src_ref=outgoing.at[slot - 1, :, where],
            dst_ref=returned.at[to_slot - 1, :, where],
            send_sem=send_sem.at[kind], recv_sem=recv_sem.at[kind, j],
            device_id=there(device), device_id_type=MESH)

    half = wide // 2
    width = heads * 128
    copies = {
        G_SIB: lambda j, s, w: moved(G_SIB, OWN, SIB, sib, j, s, w),
        G_CROSS: lambda j, s, w: moved(G_CROSS, OWN, CROSS, cross, j, s, w),
        G_TO: lambda j, s, w: moved(G_TO, OWN, FROM, to, j, s, w),
        G_FROM: lambda j, s, w: moved(G_FROM, OWN, TO, frm, j, s, w),
        G_RELAY1: lambda j, s, w: moved(G_RELAY1, CROSS, RELAY, to, j, s, w),
        G_RELAY2: lambda j, s, w: moved(G_RELAY2, TO, RELAY, cross, j, s, w),
        R_SIB: lambda j, s, w: handed(R_SIB, SIB, SIB, sib, j, s, w),
        R_EDGE: lambda j, s, w: handed(R_EDGE, EDGE, EDGE, sib, j, s, w),
        R_FROM: lambda j, s, w: handed(R_FROM, FROM, TO, frm, j, s, w),
        R_RELAY1: lambda j, s, w: handed(R_RELAY1, RELAY, RELAY, frm, j, s, w),
        R_RELAY2: lambda j, s, w: handed(R_RELAY2, RELAY, RELAY, cross, j, s, w),
        R_CROSS: lambda j, s, w: handed(R_CROSS, CROSS, CROSS, cross, j, s, w),
        R_TO: lambda j, s, w: handed(R_TO, TO, FROM, to, j, s, w),
    }

    def begin(kind, j):
        offset = half if kind in (G_RELAY2, R_RELAY2) else 0
        size = half if kind in (G_RELAY1, G_RELAY2, R_RELAY1, R_RELAY2) else wide
        copies[kind](j, j * wide + offset, size).start()

    def begin_edge(slot, j):
        moved(G_EDGE, slot, EDGE, sib, j, j * wide, wide).start()

    def await_arrival(kind, j):
        if kind == G_EDGE:
            moved(G_EDGE, CROSS, EDGE, sib, j, j * wide, wide).wait_recv()
            return
        offset = half if kind in (G_RELAY2, R_RELAY2) else 0
        size = half if kind in (G_RELAY1, G_RELAY2, R_RELAY1, R_RELAY2) else wide
        copies[kind](j, j * wide + offset, size).wait_recv()

    def send_own(j):
        begin(G_CROSS, j)
        pl.when(has_to)(lambda: begin(G_TO, j))
        pl.when(has_from)(lambda: begin(G_FROM, j))
        begin(G_SIB, j)

    def relay_on(j):
        await_arrival(G_CROSS, j)

        @pl.when(has_to)
        def _():
            begin(G_RELAY1, j)
            await_arrival(G_FROM, j)
            begin(G_RELAY2, j)

        pl.when(gives_cross)(lambda: begin_edge(CROSS, j))

    def edge_on(j):
        @pl.when(has_from)
        def _():
            await_arrival(G_RELAY1, j)
            await_arrival(G_RELAY2, j)

        pl.when(jnp.logical_not(gives_cross) & has_from)(lambda: begin_edge(RELAY, j))

    def compute(j):
        await_arrival(G_SIB, j)
        pl.when(has_from)(lambda: await_arrival(G_TO, j))
        pl.when(has_edge)(lambda: await_arrival(G_EDGE, j))
        for n in range(PACK):
            h = j * PACK + n
            where = columns(h * 128, 128)
            keys, values = kv[0, :, where], kv[1, :, where]
            asked, cotangents = buf[0, :, where], buf[1, :, where]
            norms = jnp.concatenate([stats[s, pl.ds(h, 1), :] for s in range(SLOTS)], axis=1)
            deltas = jnp.concatenate([stats[s, pl.ds(heads + h, 1), :] for s in range(SLOTS)], axis=1)
            scores = lax.dot_general(keys, asked, NT, preferred_element_type=jnp.float32)
            probs = jnp.exp(scores * factor - norms)
            dprobs = lax.dot_general(values, cotangents, NT, preferred_element_type=jnp.float32)
            dscores = (probs * (dprobs - deltas)).astype(jnp.bfloat16)
            dv = lax.dot_general(probs.astype(jnp.bfloat16), cotangents, NN,
                                 preferred_element_type=jnp.float32)
            dk = lax.dot_general(dscores, asked, NN, preferred_element_type=jnp.float32)
            dq = lax.dot_general(dscores, keys, TN, preferred_element_type=jnp.float32) * factor
            results[1, :, where] = (dk * factor).astype(jnp.bfloat16)
            results[2, :, where] = dv.astype(jnp.bfloat16)

            def part(slot):
                return dq[slot * BLK:(slot + 1) * BLK]

            for slot in (SIB, EDGE, FROM):
                outgoing[slot - 1, :, where] = part(slot).astype(jnp.bfloat16)
            own_acc[:, where] = part(OWN)
            cross_acc[:, where] = part(CROSS)
            relay_acc[:, where] = part(RELAY)
            to_acc[:, where] = part(TO)
        pl.when(has_edge)(lambda: begin(R_EDGE, j))
        pl.when(has_from)(lambda: begin(R_FROM, j))
        begin(R_SIB, j)

    def back_relay(j):
        where = columns(j * wide, wide)

        @pl.when(has_sib_edge)
        def _():
            await_arrival(R_EDGE, j)

        @pl.when(gives_cross)
        def _():
            cross_acc[:, where] += returned[EDGE - 1, :, where].astype(jnp.float32)

        @pl.when(has_from)
        def _():
            @pl.when(jnp.logical_not(gives_cross))
            def _():
                relay_acc[:, where] += returned[EDGE - 1, :, where].astype(jnp.float32)

            outgoing[RELAY - 1, :, where] = relay_acc[:, where].astype(jnp.bfloat16)
            begin(R_RELAY1, j)
            begin(R_RELAY2, j)

    def back_direct(j):
        where = columns(j * wide, wide)
        first, second = columns(j * wide, half), columns(j * wide + half, half)

        @pl.when(has_to)
        def _():
            await_arrival(R_RELAY1, j)
            await_arrival(R_RELAY2, j)
            cross_acc[:, first] += returned[RELAY - 1, :, first].astype(jnp.float32)
            to_acc[:, second] += returned[RELAY - 1, :, second].astype(jnp.float32)
            outgoing[TO - 1, :, where] = to_acc[:, where].astype(jnp.bfloat16)
            begin(R_TO, j)

        outgoing[CROSS - 1, :, where] = cross_acc[:, where].astype(jnp.bfloat16)
        begin(R_CROSS, j)

    def finish(j):
        where = columns(j * wide, wide)
        await_arrival(R_SIB, j)
        await_arrival(R_CROSS, j)
        total = own_acc[:, where] + returned[SIB - 1, :, where].astype(jnp.float32)
        own_acc[:, where] = total + returned[CROSS - 1, :, where].astype(jnp.float32)

        @pl.when(has_to)
        def _():
            await_arrival(R_FROM, j)
            own_acc[:, where] += returned[TO - 1, :, where].astype(jnp.float32)

        @pl.when(has_from)
        def _():
            await_arrival(R_TO, j)
            own_acc[:, where] += returned[FROM - 1, :, where].astype(jnp.float32)

        results[0, :, where] = own_acc[:, where].astype(jnp.bfloat16)

    loads[0].wait()
    loads[1].wait()
    ahead = 2
    for j in range(ahead):
        send_own(j)
    loads[2].wait()
    loads[3].wait()
    stats[OWN] = stats_in[...]
    for slot, device, present in places:
        guarded(present, lambda slot=slot, device=device: stat_copy(mirror[slot], device).wait_recv())
    for slot in range(SLOTS):
        stats[slot, pl.ds(0, heads), :] += bias_ref[pl.ds(slot, 1), :]

    def step(t, carry):
        for lag, action in ((-ahead, send_own), (1, relay_on), (2, edge_on), (6, finish),
                            (5, back_direct), (4, back_relay), (3, compute)):
            j = t - lag
            pl.when((j >= max(0, -lag * (lag < 0))) & (j < chunks))(functools.partial(action, j))
        return carry

    lax.fori_loop(0, chunks + 6, step, 0)

    stores = [pltpu.make_async_copy(results.at[n], target, local_sem.at[n])
              for n, target in enumerate((dq_hbm, dk_hbm, dv_hbm))]
    for store in stores:
        store.start()
    for slot, device, present in places:
        guarded(present, lambda slot=slot, device=device: stat_copy(slot, device).wait_send())
    for kind, present in ((G_SIB, None), (G_CROSS, None), (G_TO, has_to), (G_FROM, has_from),
                          (G_RELAY1, has_to), (G_RELAY2, has_to), (R_SIB, None), (R_EDGE, has_edge),
                          (R_FROM, has_from), (R_RELAY1, has_from), (R_RELAY2, has_from),
                          (R_CROSS, None), (R_TO, has_to)):
        size = width // 2 if kind in (G_RELAY1, G_RELAY2, R_RELAY1, R_RELAY2) else width
        guarded(present, lambda kind=kind, size=size: copies[kind](0, 0, size).wait_send())
    pl.when(has_sib_edge)(lambda: moved(G_EDGE, CROSS, EDGE, sib, 0, 0, width).wait_send())
    for store in stores:
        store.wait()


def per_device(queries, key_states, value_states, out_grads, log_norms, row_deltas, kv_blocks):
    tok_rows, width = queries.shape
    heads = log_norms.shape[0]
    devices = lax.axis_size("ctx")
    me = lax.axis_index("ctx")
    sign = 1 - 2 * ((me // 2) % 2)
    core = me % 2
    asking = jnp.stack([me, me + 1 - 2 * core, me + 2 * sign, me - 2 * sign, me + 2 * core - 1,
                        me + 4 * sign, me - 4 * sign, me])
    inside = (asking >= 0) & (asking < devices)
    rows = kv_blocks[jnp.clip(asking, 0, devices - 1)]
    listed = jnp.any(rows == me, axis=1) & inside
    bias = jnp.broadcast_to(jnp.where(listed, 0.0, FAR).astype(jnp.float32)[:, None], (8, BLK))
    stats = jnp.concatenate([log_norms, row_deltas]).astype(jnp.float32)
    chunks = heads // PACK
    anywhere = pl.BlockSpec(memory_space=pl.ANY)
    in_vmem = pl.BlockSpec(memory_space=pltpu.VMEM)
    out = jax.ShapeDtypeStruct((tok_rows, width), jnp.bfloat16)
    return pl.pallas_call(
        functools.partial(kernel, devices, heads),
        out_shape=(out, out, out),
        in_specs=[anywhere] * 4 + [in_vmem] * 2,
        out_specs=(anywhere,) * 3,
        scratch_shapes=[
            pltpu.VMEM((2, SLOTS * BLK, width), jnp.bfloat16),
            pltpu.VMEM((2, BLK, width), jnp.bfloat16),
            pltpu.VMEM((SLOTS, 2 * heads, BLK), jnp.float32),
            pltpu.VMEM((BLK, width), jnp.float32),
            pltpu.VMEM((BLK, width), jnp.float32),
            pltpu.VMEM((BLK, width), jnp.float32),
            pltpu.VMEM((BLK, width), jnp.float32),
            pltpu.VMEM((SLOTS - 1, BLK, width), jnp.bfloat16),
            pltpu.VMEM((SLOTS - 1, BLK, width), jnp.bfloat16),
            pltpu.VMEM((3, BLK, width), jnp.bfloat16),
            pltpu.SemaphoreType.DMA((KINDS,)),
            pltpu.SemaphoreType.DMA((KINDS, chunks)),
            pltpu.SemaphoreType.DMA((SLOTS,)),
            pltpu.SemaphoreType.DMA((SLOTS,)),
            pltpu.SemaphoreType.DMA((4,)),
        ],
        compiler_params=pltpu.CompilerParams(
            collective_id=0, has_side_effects=True, vmem_limit_bytes=50 * 1024 * 1024),
        cost_estimate=pl.CostEstimate(
            flops=10 * heads * SLOTS * BLK * BLK * 128, bytes_accessed=14 * tok_rows * width,
            transcendentals=heads * SLOTS * BLK * BLK),
    )(queries, key_states, value_states, out_grads, stats, bias)


def solution(mesh):
    rows = P(("groups", "ctx"), None)
    lanes = P(None, ("groups", "ctx"))
    return jax.shard_map(
        per_device,
        mesh=mesh,
        in_specs=(rows, rows, rows, rows, lanes, lanes, P()),
        out_specs=(rows, rows, rows),
        check_vma=False,
    )
```

time: 359 us -> 91.8 us (0.26)
  the two profiles are of different devices: /device:TPU:1 before, /device:TPU:0 now
where the time goes in v1:
time: 91.8 us; the launch traced here: 91.5 us
  Pallas kernels  82.9 us (90%)
  local copies, waits for them, and re-layouts  7.75 us (8%)
    pallas_call x1, Pallas kernels, per_device(): pl.pallas_call(functools.partial(kernel, devices, heads), out_shape=(out,...  82.9 us
    unnamed x16, local copies, waits for them, and re-layouts  6.93 us

profile of v1, /device:TPU:0, one launch (start us, length us, event | category | flops | bytes accessed | tf_op | source)
XLA Modules:
  0.0 91.5 jit_solution(15650834404010221091)
XLA Ops:
  0.7 0.1 stack.48
  0.8 0.0 copy-start.5
  0.8 0.1 stack.56
  0.9 0.6 copy-done.5
  1.5 0.1 copy.10
  1.6 0.0 copy-start.4
  1.6 0.6 gather_fusion
  2.1 0.0 copy-start.3
  2.1 0.1 compare_reduce_fusion
  2.3 0.1 broadcast_in_dim.17.bias_ref
  2.3 0.0 copy-done.4
  2.3 0.5 copy-done.3
  2.8 0.0 copy-start
  2.8 1.1 %copy-done = bf16[128,2560]{1,0:T(8,128)(2,1)S(1)} copy-done((bf16[128,2560]{1,0:T(8,128)(2,1)S(1)}, bf16[128,2560]{1,0:T(8,128)(2,1)}, u32[]{:S(2)}) %copy-start) | copy-done | bytes 655384
  3.9 0.0 copy-start.1
  3.9 1.1 %copy-done.1 = bf16[128,2560]{1,0:T(8,128)(2,1)S(1)} copy-done((bf16[128,2560]{1,0:T(8,128)(2,1)S(1)}, bf16[128,2560]{1,0:T(8,128)(2,1)}, u32[]{:S(2)}) %copy-start.1) | copy-done | bytes 655384
  5.0 0.0 copy-start.2
  5.0 1.1 %copy-done.2 = bf16[128,2560]{1,0:T(8,128)(2,1)S(1)} copy-done((bf16[128,2560]{1,0:T(8,128)(2,1)S(1)}, bf16[128,2560]{1,0:T(8,128)(2,1)}, u32[]{:S(2)}) %copy-start.2) | copy-done | bytes 655384
  6.1 82.9 %shard_map.94 = (bf16[128,2560]{1,0:T(8,128)(2,1)S(1)}, bf16[128,2560]{1,0:T(8,128)(2,1)S(1)}, bf16[128,2560]{1,0:T(8,128)(2,1)S(1)}) custom-call(bf16[128,2560]{1,0:T(8,128)(2,1)S(1)} %copy-done, bf16[128,2560]{1,0:T(8,128)(2,1)S(1)} %copy-done.1, bf16[128,2560]{1,0:T(8,128)(2,1)S(1)} %copy-done.2, bf16[128,2560]{1,0:T(8,128)(2,1)} %g_hbm.1, ...), custom_call_target="tpu_custom_call" | custom-call | flops 2936012800 | bytes 4587520 | tf_op jit(solution)/shard_map/pallas_call | solution.py:318
  89.0 0.8 copy.14
  89.8 0.8 copy.15
  90.7 0.8 copy.16
  (4 shorter events, 0.0 us)
Async XLA Ops:
  0.8 0.7 copy-start.5
  1.6 0.8 copy-start.4
  2.1 0.7 copy-start.3
  2.8 1.1 %copy-start = (bf16[128,2560]{1,0:T(8,128)(2,1)S(1)}, bf16[128,2560]{1,0:T(8,128)(2,1)}, u32[]{:S(2)}) copy-start(bf16[128,2560]{1,0:T(8,128)(2,1)} %q_hbm.1) | copy-start | bytes 1966084
  3.9 1.1 %copy-start.1 = (bf16[128,2560]{1,0:T(8,128)(2,1)S(1)}, bf16[128,2560]{1,0:T(8,128)(2,1)}, u32[]{:S(2)}) copy-start(bf16[128,2560]{1,0:T(8,128)(2,1)} %k_hbm.1) | copy-start | bytes 1966084
  5.0 1.1 %copy-start.2 = (bf16[128,2560]{1,0:T(8,128)(2,1)S(1)}, bf16[128,2560]{1,0:T(8,128)(2,1)}, u32[]{:S(2)}) copy-start(bf16[128,2560]{1,0:T(8,128)(2,1)} %v_hbm.1) | copy-start | bytes 1966084

commit v2 on v1

--- a/solution.py
+++ b/solution.py
@@ -14,16 +14,20 @@
 OWN, SIB, CROSS, RELAY, EDGE, TO, FROM = range(7)
 SLOTS = 7
 (G_SIB, G_CROSS, G_TO, G_FROM, G_RELAY1, G_RELAY2, G_EDGE,
- R_SIB, R_EDGE, R_FROM, R_RELAY1, R_RELAY2, R_CROSS, R_TO) = range(14)
-KINDS = 14
+ R_SIB, R_EDGE, R_FROM, R_RELAY, R_CROSS, R_TO) = range(13)
+KINDS = 13
+AHEAD = 4
+RELAY_LAG, EDGE_LAG, COMPUTE_LAG, BACK_RELAY_LAG, BACK_LAG, FINISH_LAG = 1, 3, 4, 5, 7, 9
+DELTA_ROW = 24
 NN = (((1,), (0,)), ((), ()))
 NT = (((1,), (1,)), ((), ()))
 TN = (((0,), (0,)), ((), ()))
 MESH = pl.DeviceIdType.MESH
 
 
-def kernel(devices, heads, q_hbm, k_hbm, v_hbm, g_hbm, stats_in, bias_ref, dq_hbm, dk_hbm, dv_hbm,
-           buf, kv, stats, own_acc, cross_acc, relay_acc, to_acc, outgoing, returned, results,
+def kernel(devices, heads, q_hbm, k_hbm, v_hbm, g_hbm, norms_ref, deltas_ref, lists_ref,
+           dq_hbm, dk_hbm, dv_hbm,
+           buf, kv, stats, own_acc, cross_acc, relay_acc, outgoing, returned, results,
            send_sem, recv_sem, stat_send, stat_recv, local_sem):
     group = lax.axis_index("groups")
     me = lax.axis_index("ctx")
@@ -66,6 +70,9 @@
         load.start()
 
     barrier = pltpu.get_barrier_semaphore()
+    stats[OWN] = jnp.zeros(stats.shape[1:], stats.dtype)
+    stats[OWN, 0:heads, :] = norms_ref[...].astype(jnp.float32)
+    stats[OWN, DELTA_ROW:DELTA_ROW + heads, :] = deltas_ref[...].astype(jnp.float32)
     for _, device, present in places:
         guarded(present, lambda device=device: pl.semaphore_signal(
             barrier, inc=1, device_id=there(device), device_id_type=MESH))
@@ -83,11 +90,9 @@
 
     def stat_copy(slot, device):
         return pltpu.make_async_remote_copy(
-            src_ref=stats_in, dst_ref=stats.at[mirror[slot]], send_sem=stat_send.at[slot],
+            src_ref=stats.at[OWN], dst_ref=stats.at[mirror[slot]], send_sem=stat_send.at[slot],
             recv_sem=stat_recv.at[mirror[slot]], device_id=there(device), device_id_type=MESH)
 
-    for slot, device, present in places:
-        guarded(present, lambda slot=slot, device=device: stat_copy(slot, device).start())
 
     def columns(start, size):
         return pl.ds(pl.multiple_of(start, 128), size)
@@ -120,15 +125,14 @@
         R_SIB: lambda j, s, w: handed(R_SIB, SIB, SIB, sib, j, s, w),
         R_EDGE: lambda j, s, w: handed(R_EDGE, EDGE, EDGE, sib, j, s, w),
         R_FROM: lambda j, s, w: handed(R_FROM, FROM, TO, frm, j, s, w),
-        R_RELAY1: lambda j, s, w: handed(R_RELAY1, RELAY, RELAY, frm, j, s, w),
-        R_RELAY2: lambda j, s, w: handed(R_RELAY2, RELAY, RELAY, cross, j, s, w),
+        R_RELAY: lambda j, s, w: handed(R_RELAY, RELAY, RELAY, frm, j, s, w),
         R_CROSS: lambda j, s, w: handed(R_CROSS, CROSS, CROSS, cross, j, s, w),
         R_TO: lambda j, s, w: handed(R_TO, TO, FROM, to, j, s, w),
     }
 
     def begin(kind, j):
-        offset = half if kind in (G_RELAY2, R_RELAY2) else 0
-        size = half if kind in (G_RELAY1, G_RELAY2, R_RELAY1, R_RELAY2) else wide
+        offset = half if kind == G_RELAY2 else 0
+        size = half if kind in (G_RELAY1, G_RELAY2) else wide
         copies[kind](j, j * wide + offset, size).start()
 
     def begin_edge(slot, j):
@@ -138,8 +142,8 @@
         if kind == G_EDGE:
             moved(G_EDGE, CROSS, EDGE, sib, j, j * wide, wide).wait_recv()
             return
-        offset = half if kind in (G_RELAY2, R_RELAY2) else 0
-        size = half if kind in (G_RELAY1, G_RELAY2, R_RELAY1, R_RELAY2) else wide
+        offset = half if kind == G_RELAY2 else 0
+        size = half if kind in (G_RELAY1, G_RELAY2) else wide
         copies[kind](j, j * wide + offset, size).wait_recv()
 
     def send_own(j):
@@ -177,7 +181,7 @@
             keys, values = kv[0, :, where], kv[1, :, where]
             asked, cotangents = buf[0, :, where], buf[1, :, where]
             norms = jnp.concatenate([stats[s, pl.ds(h, 1), :] for s in range(SLOTS)], axis=1)
-            deltas = jnp.concatenate([stats[s, pl.ds(heads + h, 1), :] for s in range(SLOTS)], axis=1)
+            deltas = jnp.concatenate([stats[s, pl.ds(DELTA_ROW + h, 1), :] for s in range(SLOTS)], axis=1)
             scores = lax.dot_general(keys, asked, NT, preferred_element_type=jnp.float32)
             probs = jnp.exp(scores * factor - norms)
             dprobs = lax.dot_general(values, cotangents, NT, preferred_element_type=jnp.float32)
@@ -192,14 +196,14 @@
             def part(slot):
                 return dq[slot * BLK:(slot + 1) * BLK]
 
-            for slot in (SIB, EDGE, FROM):
+            for slot in (SIB, EDGE, FROM, TO):
                 outgoing[slot - 1, :, where] = part(slot).astype(jnp.bfloat16)
             own_acc[:, where] = part(OWN)
             cross_acc[:, where] = part(CROSS)
             relay_acc[:, where] = part(RELAY)
-            to_acc[:, where] = part(TO)
         pl.when(has_edge)(lambda: begin(R_EDGE, j))
         pl.when(has_from)(lambda: begin(R_FROM, j))
+        pl.when(has_to)(lambda: begin(R_TO, j))
         begin(R_SIB, j)
 
     def back_relay(j):
@@ -220,21 +224,15 @@
                 relay_acc[:, where] += returned[EDGE - 1, :, where].astype(jnp.float32)
 
             outgoing[RELAY - 1, :, where] = relay_acc[:, where].astype(jnp.bfloat16)
-            begin(R_RELAY1, j)
-            begin(R_RELAY2, j)
+            begin(R_RELAY, j)
 
     def back_direct(j):
         where = columns(j * wide, wide)
-        first, second = columns(j * wide, half), columns(j * wide + half, half)
 
         @pl.when(has_to)
         def _():
-            await_arrival(R_RELAY1, j)
-            await_arrival(R_RELAY2, j)
-            cross_acc[:, first] += returned[RELAY - 1, :, first].astype(jnp.float32)
-            to_acc[:, second] += returned[RELAY - 1, :, second].astype(jnp.float32)
-            outgoing[TO - 1, :, where] = to_acc[:, where].astype(jnp.bfloat16)
-            begin(R_TO, j)
+            await_arrival(R_RELAY, j)
+            cross_acc[:, where] += returned[RELAY - 1, :, where].astype(jnp.float32)
 
         outgoing[CROSS - 1, :, where] = cross_acc[:, where].astype(jnp.bfloat16)
         begin(R_CROSS, j)
@@ -260,37 +258,43 @@
 
     loads[0].wait()
     loads[1].wait()
-    ahead = 2
-    for j in range(ahead):
+    for j in range(AHEAD):
         send_own(j)
+    for slot, device, present in places:
+        guarded(present, lambda slot=slot, device=device: stat_copy(slot, device).start())
     loads[2].wait()
     loads[3].wait()
-    stats[OWN] = stats_in[...]
     for slot, device, present in places:
         guarded(present, lambda slot=slot, device=device: stat_copy(mirror[slot], device).wait_recv())
-    for slot in range(SLOTS):
-        stats[slot, pl.ds(0, heads), :] += bias_ref[pl.ds(slot, 1), :]
+        guarded(present, lambda slot=slot, device=device: stat_copy(slot, device).wait_send())
+    for slot, device, present in places:
+        asking = device if present is None else jnp.where(present, device, 0)
+        listed = lists_ref[0, asking] == me
+        for n in range(1, lists_ref.shape[0]):
+            listed = listed | (lists_ref[n, asking] == me)
+        if present is not None:
+            listed = listed & present
+        stats[slot, 0:heads, :] += jnp.where(listed, 0.0, FAR)
 
     def step(t, carry):
-        for lag, action in ((-ahead, send_own), (1, relay_on), (2, edge_on), (6, finish),
-                            (5, back_direct), (4, back_relay), (3, compute)):
+        for lag, action in ((-AHEAD, send_own), (RELAY_LAG, relay_on), (EDGE_LAG, edge_on),
+                            (FINISH_LAG, finish), (BACK_LAG, back_direct), (BACK_RELAY_LAG, back_relay),
+                            (COMPUTE_LAG, compute)):
             j = t - lag
-            pl.when((j >= max(0, -lag * (lag < 0))) & (j < chunks))(functools.partial(action, j))
+            pl.when((j >= max(0, -lag)) & (j < chunks))(functools.partial(action, j))
         return carry
 
-    lax.fori_loop(0, chunks + 6, step, 0)
+    lax.fori_loop(0, chunks + FINISH_LAG, step, 0)
 
     stores = [pltpu.make_async_copy(results.at[n], target, local_sem.at[n])
               for n, target in enumerate((dq_hbm, dk_hbm, dv_hbm))]
     for store in stores:
         store.start()
-    for slot, device, present in places:
-        guarded(present, lambda slot=slot, device=device: stat_copy(slot, device).wait_send())
     for kind, present in ((G_SIB, None), (G_CROSS, None), (G_TO, has_to), (G_FROM, has_from),
                           (G_RELAY1, has_to), (G_RELAY2, has_to), (R_SIB, None), (R_EDGE, has_edge),
-                          (R_FROM, has_from), (R_RELAY1, has_from), (R_RELAY2, has_from),
+                          (R_FROM, has_from), (R_RELAY, has_from),
                           (R_CROSS, None), (R_TO, has_to)):
-        size = width // 2 if kind in (G_RELAY1, G_RELAY2, R_RELAY1, R_RELAY2) else width
+        size = width // 2 if kind in (G_RELAY1, G_RELAY2) else width
         guarded(present, lambda kind=kind, size=size: copies[kind](0, 0, size).wait_send())
     pl.when(has_sib_edge)(lambda: moved(G_EDGE, CROSS, EDGE, sib, 0, 0, width).wait_send())
     for store in stores:
@@ -301,16 +305,6 @@
     tok_rows, width = queries.shape
     heads = log_norms.shape[0]
     devices = lax.axis_size("ctx")
-    me = lax.axis_index("ctx")
-    sign = 1 - 2 * ((me // 2) % 2)
-    core = me % 2
-    asking = jnp.stack([me, me + 1 - 2 * core, me + 2 * sign, me - 2 * sign, me + 2 * core - 1,
-                        me + 4 * sign, me - 4 * sign, me])
-    inside = (asking >= 0) & (asking < devices)
-    rows = kv_blocks[jnp.clip(asking, 0, devices - 1)]
-    listed = jnp.any(rows == me, axis=1) & inside
-    bias = jnp.broadcast_to(jnp.where(listed, 0.0, FAR).astype(jnp.float32)[:, None], (8, BLK))
-    stats = jnp.concatenate([log_norms, row_deltas]).astype(jnp.float32)
     chunks = heads // PACK
     anywhere = pl.BlockSpec(memory_space=pl.ANY)
     in_vmem = pl.BlockSpec(memory_space=pltpu.VMEM)
@@ -318,13 +312,12 @@
     return pl.pallas_call(
         functools.partial(kernel, devices, heads),
         out_shape=(out, out, out),
-        in_specs=[anywhere] * 4 + [in_vmem] * 2,
+        in_specs=[anywhere] * 4 + [in_vmem] * 2 + [pl.BlockSpec(memory_space=pltpu.SMEM)],
         out_specs=(anywhere,) * 3,
         scratch_shapes=[
             pltpu.VMEM((2, SLOTS * BLK, width), jnp.bfloat16),
             pltpu.VMEM((2, BLK, width), jnp.bfloat16),
-            pltpu.VMEM((SLOTS, 2 * heads, BLK), jnp.float32),
-            pltpu.VMEM((BLK, width), jnp.float32),
+            pltpu.VMEM((SLOTS, 2 * DELTA_ROW, BLK), jnp.float32),
             pltpu.VMEM((BLK, width), jnp.float32),
             pltpu.VMEM((BLK, width), jnp.float32),
             pltpu.VMEM((BLK, width), jnp.float32),
@@ -338,11 +331,11 @@
             pltpu.SemaphoreType.DMA((4,)),
         ],
         compiler_params=pltpu.CompilerParams(
-            collective_id=0, has_side_effects=True, vmem_limit_bytes=50 * 1024 * 1024),
+            collective_id=0, has_side_effects=True, vmem_limit_bytes=62 * 1024 * 1024),
         cost_estimate=pl.CostEstimate(
             flops=10 * heads * SLOTS * BLK * BLK * 128, bytes_accessed=14 * tok_rows * width,
             transcendentals=heads * SLOTS * BLK * BLK),
-    )(queries, key_states, value_states, out_grads, stats, bias)
+    )(queries, key_states, value_states, out_grads, log_norms, row_deltas, kv_blocks.T)
 
 
 def solution(mesh):

time: 91.8 us -> 79.8 us (0.87)
  Pallas kernels: 82.9 us -> 74.7 us
  local copies, waits for them, and re-layouts: 7.75 us -> 4.19 us
    pallas_call x1, Pallas kernels: 82.9 us -> 74.7 us  [per_device(): pl.pallas_call(functools.partial(kernel, devices, heads), out_shape=(out,...]
    unnamed x16 -> x7, local copies, waits for them, and re-layouts: 6.93 us -> 4.19 us
where the time goes in v2:
time: 79.8 us; the launch traced here: 79.6 us
  Pallas kernels  74.7 us (94%)
  local copies, waits for them, and re-layouts  4.19 us (5%)
    pallas_call x1, Pallas kernels, per_device(): pl.pallas_call(functools.partial(kernel, devices, heads), out_shape=(out,...  74.7 us
    unnamed x7, local copies, waits for them, and re-layouts  4.19 us

profile of v2, /device:TPU:0, one launch (start us, length us, event | category | flops | bytes accessed | tf_op | source)
XLA Modules:
  0.0 79.6 jit_solution(13829617847502553453)
XLA Ops:
  0.6 74.7 %shard_map.94 = (bf16[128,2560]{1,0:T(8,128)(2,1)}, bf16[128,2560]{1,0:T(8,128)(2,1)}, bf16[128,2560]{1,0:T(8,128)(2,1)}) custom-call(bf16[128,2560]{1,0:T(8,128)(2,1)} %q_hbm.1, bf16[128,2560]{1,0:T(8,128)(2,1)} %k_hbm.1, bf16[128,2560]{1,0:T(8,128)(2,1)} %v_hbm.1, bf16[128,2560]{1,0:T(8,128)(2,1)} %g_hbm.1, bf16[20,128]{1,0:T(8,128)(2,1)} %norms_ref.1, ...), custom_call_target="tpu_custom_call" | custom-call | flops 2936012800 | bytes 4587520 | tf_op jit(solution)/shard_map/pallas_call | solution.py:312
  75.4 0.0 copy-start.1
  75.4 2.0 %copy.13 = bf16[128,2560]{1,0:T(8,128)(2,1)} copy(bf16[128,2560]{1,0:T(8,128)(2,1)} %get-tuple-element.6) | data formatting | bytes 1310720
  77.4 0.0 copy-done.1
  77.4 0.0 copy-start
  77.4 0.8 %copy.14 = bf16[128,2560]{1,0:T(8,128)(2,1)} copy(bf16[128,2560]{1,0:T(8,128)(2,1)S(1)} %copy-done.1) | data formatting | bytes 1310720
  78.2 0.5 copy-done
  78.7 0.8 %copy.15 = bf16[128,2560]{1,0:T(8,128)(2,1)} copy(bf16[128,2560]{1,0:T(8,128)(2,1)S(1)} %copy-done) | data formatting | bytes 1310720
Async XLA Ops:
  75.4 2.0 %copy-start.1 = (bf16[128,2560]{1,0:T(8,128)(2,1)S(1)}, bf16[128,2560]{1,0:T(8,128)(2,1)}, u32[]{:S(2)}) copy-start(bf16[128,2560]{1,0:T(8,128)(2,1)} %get-tuple-element.7) | copy-start | bytes 1966084
  77.4 1.3 %copy-start = (bf16[128,2560]{1,0:T(8,128)(2,1)S(1)}, bf16[128,2560]{1,0:T(8,128)(2,1)}, u32[]{:S(2)}) copy-start(bf16[128,2560]{1,0:T(8,128)(2,1)} %get-tuple-element.8) | copy-start | bytes 1966084

commit v3 on v2

--- a/solution.py
+++ b/solution.py
@@ -18,6 +18,7 @@
 KINDS = 13
 AHEAD = 4
 RELAY_LAG, EDGE_LAG, COMPUTE_LAG, BACK_RELAY_LAG, BACK_LAG, FINISH_LAG = 1, 3, 4, 5, 7, 9
+PIECES = 4
 DELTA_ROW = 24
 NN = (((1,), (0,)), ((), ()))
 NT = (((1,), (1,)), ((), ()))
@@ -28,7 +29,7 @@
 def kernel(devices, heads, q_hbm, k_hbm, v_hbm, g_hbm, norms_ref, deltas_ref, lists_ref,
            dq_hbm, dk_hbm, dv_hbm,
            buf, kv, stats, own_acc, cross_acc, relay_acc, outgoing, returned, results,
-           send_sem, recv_sem, stat_send, stat_recv, local_sem):
+           send_sem, recv_sem, stat_send, stat_recv, local_sem, store_sem):
     group = lax.axis_index("groups")
     me = lax.axis_index("ctx")
     chunks = heads // PACK
@@ -145,6 +146,10 @@
         offset = half if kind == G_RELAY2 else 0
         size = half if kind in (G_RELAY1, G_RELAY2) else wide
         copies[kind](j, j * wide + offset, size).wait_recv()
+
+    def store(n, target, start, size):
+        where = columns(start, size)
+        return pltpu.make_async_copy(results.at[n, :, where], target.at[:, where], store_sem.at[n])
 
     def send_own(j):
         begin(G_CROSS, j)
@@ -206,6 +211,9 @@
         pl.when(has_to)(lambda: begin(R_TO, j))
         begin(R_SIB, j)
 
+        for n, target in ((1, dk_hbm), (2, dv_hbm)):
+            store(n, target, j * wide, wide).start()
+
     def back_relay(j):
         where = columns(j * wide, wide)
 
@@ -255,6 +263,7 @@
             own_acc[:, where] += returned[FROM - 1, :, where].astype(jnp.float32)
 
         results[0, :, where] = own_acc[:, where].astype(jnp.bfloat16)
+        store(0, dq_hbm, j * wide, wide).start()
 
     loads[0].wait()
     loads[1].wait()
@@ -277,19 +286,14 @@
         stats[slot, 0:heads, :] += jnp.where(listed, 0.0, FAR)
 
     def step(t, carry):
-        for lag, action in ((-AHEAD, send_own), (RELAY_LAG, relay_on), (EDGE_LAG, edge_on),
-                            (FINISH_LAG, finish), (BACK_LAG, back_direct), (BACK_RELAY_LAG, back_relay),
-                            (COMPUTE_LAG, compute)):
+        for lag, action in ((RELAY_LAG, relay_on), (EDGE_LAG, edge_on), (BACK_LAG, back_direct), (BACK_RELAY_LAG, back_relay), (COMPUTE_LAG, compute),
+                            (-AHEAD, send_own), (FINISH_LAG, finish)):
             j = t - lag
             pl.when((j >= max(0, -lag)) & (j < chunks))(functools.partial(action, j))
         return carry
 
     lax.fori_loop(0, chunks + FINISH_LAG, step, 0)
 
-    stores = [pltpu.make_async_copy(results.at[n], target, local_sem.at[n])
-              for n, target in enumerate((dq_hbm, dk_hbm, dv_hbm))]
-    for store in stores:
-        store.start()
     for kind, present in ((G_SIB, None), (G_CROSS, None), (G_TO, has_to), (G_FROM, has_from),
                           (G_RELAY1, has_to), (G_RELAY2, has_to), (R_SIB, None), (R_EDGE, has_edge),
                           (R_FROM, has_from), (R_RELAY, has_from),
@@ -297,8 +301,25 @@
         size = width // 2 if kind in (G_RELAY1, G_RELAY2) else width
         guarded(present, lambda kind=kind, size=size: copies[kind](0, 0, size).wait_send())
     pl.when(has_sib_edge)(lambda: moved(G_EDGE, CROSS, EDGE, sib, 0, 0, width).wait_send())
-    for store in stores:
-        store.wait()
+    for n, target in enumerate((dq_hbm, dk_hbm, dv_hbm)):
+        store(n, target, 0, width).wait()
+
+
+def keep(dq_in, dk_in, dv_in, dq_out, dk_out, dv_out, held, in_sem, out_sem):
+    size = held.shape[1] // PIECES
+    arrays = ((dq_in, dq_out), (dk_in, dk_out), (dv_in, dv_out))
+    pieces = [(n, p, pl.ds(p * size, size)) for p in range(PIECES) for n in range(3)]
+    into = {(n, p): pltpu.make_async_copy(arrays[n][0].at[rows], held.at[n, rows], in_sem.at[n, p])
+            for n, p, rows in pieces}
+    out = {(n, p): pltpu.make_async_copy(held.at[n, rows], arrays[n][1].at[rows], out_sem.at[n, p])
+           for n, p, rows in pieces}
+    for n, p, _ in pieces:
+        into[n, p].start()
+    for n, p, _ in pieces:
+        into[n, p].wait()
+        out[n, p].start()
+    for n, p, _ in pieces:
+        out[n, p].wait()
 
 
 def per_device(queries, key_states, value_states, out_grads, log_norms, row_deltas, kv_blocks):
@@ -309,7 +330,7 @@
     anywhere = pl.BlockSpec(memory_space=pl.ANY)
     in_vmem = pl.BlockSpec(memory_space=pltpu.VMEM)
     out = jax.ShapeDtypeStruct((tok_rows, width), jnp.bfloat16)
-    return pl.pallas_call(
+    grads = pl.pallas_call(
         functools.partial(kernel, devices, heads),
         out_shape=(out, out, out),
         in_specs=[anywhere] * 4 + [in_vmem] * 2 + [pl.BlockSpec(memory_space=pltpu.SMEM)],
@@ -329,6 +350,7 @@
             pltpu.SemaphoreType.DMA((SLOTS,)),
             pltpu.SemaphoreType.DMA((SLOTS,)),
             pltpu.SemaphoreType.DMA((4,)),
+            pltpu.SemaphoreType.DMA((3,)),
         ],
         compiler_params=pltpu.CompilerParams(
             collective_id=0, has_side_effects=True, vmem_limit_bytes=62 * 1024 * 1024),
@@ -336,6 +358,19 @@
             flops=10 * heads * SLOTS * BLK * BLK * 128, bytes_accessed=14 * tok_rows * width,
             transcendentals=heads * SLOTS * BLK * BLK),
     )(queries, key_states, value_states, out_grads, log_norms, row_deltas, kv_blocks.T)
+    return pl.pallas_call(
+        keep,
+        out_shape=(out, out, out),
+        in_specs=[anywhere] * 3,
+        out_specs=(anywhere,) * 3,
+        scratch_shapes=[
+            pltpu.VMEM((3, BLK, width), jnp.bfloat16),
+            pltpu.SemaphoreType.DMA((3, PIECES)),
+            pltpu.SemaphoreType.DMA((3, PIECES)),
+        ],
+        compiler_params=pltpu.CompilerParams(vmem_limit_bytes=62 * 1024 * 1024),
+        cost_estimate=pl.CostEstimate(flops=0, bytes_accessed=12 * tok_rows * width, transcendentals=0),
+    )(*grads)
 
 
 def solution(mesh):

time: 79.8 us -> 76.8 us (0.962)
  local copies, waits for them, and re-layouts: 4.19 us -> 0 us
  Pallas kernels: 74.7 us -> 75.5 us
    unnamed x7 -> x0, local copies, waits for them, and re-layouts: 4.19 us -> none
    pallas_call x0 -> x1, Pallas kernels: none -> 2.49 us  [per_device(): pl.pallas_call(keep, out_shape=(out, out, out), in_specs=[anywhere] * 3,...]
    pallas_call x1, Pallas kernels: 74.7 us -> 73 us  [per_device(): pl.pallas_call(functools.partial(kernel, devices, heads), out_shape=(out,...]
where the time goes in v3:
time: 76.8 us; the launch traced here: 76.2 us
  Pallas kernels  75.5 us (98%)
    pallas_call x1, Pallas kernels, per_device(): pl.pallas_call(functools.partial(kernel, devices, heads), out_shape=(out,...  73 us
    pallas_call x1, Pallas kernels, per_device(): pl.pallas_call(keep, out_shape=(out, out, out), in_specs=[anywhere] * 3,...  2.49 us

profile of v3, /device:TPU:0, one launch (start us, length us, event | category | flops | bytes accessed | tf_op | source)
XLA Modules:
  0.0 76.2 jit_solution(13053221831849299073)
XLA Ops:
  0.6 73.0 %shard_map.94 = (bf16[128,2560]{1,0:T(8,128)(2,1)}, bf16[128,2560]{1,0:T(8,128)(2,1)}, bf16[128,2560]{1,0:T(8,128)(2,1)}) custom-call(bf16[128,2560]{1,0:T(8,128)(2,1)} %q_hbm.1, bf16[128,2560]{1,0:T(8,128)(2,1)} %k_hbm.1, bf16[128,2560]{1,0:T(8,128)(2,1)} %v_hbm.1, bf16[128,2560]{1,0:T(8,128)(2,1)} %g_hbm.1, bf16[20,128]{1,0:T(8,128)(2,1)} %norms_ref.1, ...), custom_call_target="tpu_custom_call" | custom-call | flops 2936012800 | bytes 4587520 | tf_op jit(solution)/shard_map/pallas_call | solution.py:333
  73.7 2.5 %shard_map.95 = (bf16[128,2560]{1,0:T(8,128)(2,1)}, bf16[128,2560]{1,0:T(8,128)(2,1)}, bf16[128,2560]{1,0:T(8,128)(2,1)}) custom-call(bf16[128,2560]{1,0:T(8,128)(2,1)} %get-tuple-element.6.dq_in, bf16[128,2560]{1,0:T(8,128)(2,1)} %get-tuple-element.7.dk_in, bf16[128,2560]{1,0:T(8,128)(2,1)} %get-tuple-element.8.dv_in), custom_call_target="tpu_custom_call" | custom-call | bytes 3932160 | tf_op jit(solution)/shard_map/pallas_call | solution.py:361
